TPU v7x, 32 devices: a whole 2x2x4 slice. The times are simulated.
32 devices in a mesh: seq: 8 (over z, x), head: 4 (over y, core).
Axes of the slice: x: 2, y: 2, z: 4, core: 2. Of those that a mesh axis runs over, the one named last changes fastest.
Arguments:
- queries: bfloat16 [4096, 16, 128], P('seq', 'head'), may hold values from -6 to 6
- keys: bfloat16 [4096, 16, 128], P('seq', 'head'), may hold values from -6 to 6
- values: bfloat16 [4096, 16, 256], P('seq', 'head'), may hold values from -15 to 15
- beta: float32 [16, 4096], P('head', 'seq'), may hold values from 0 to 0.9
- reset_blocks: int32 [8, 2], P('seq'), may hold values from 0 to 4, as said below
- out_weight: bfloat16 [4096, 4096], P('head'), may hold values from -0.09375 to 0.09375
Outputs:
- layer_out: bfloat16 [4096, 4096], P(('seq', 'head'))
Inputs may be any that keep to these rules, and one draw needn't show every extreme that they name: `reset_blocks`: row s lists distinct local indices (0 to 3) of the blocks of sequence shard s at which an episode begins; unused slots hold 4.
All inputs are finite; a program needn't handle non-finite values.
Results may differ from a plain program's by a relative error of at most 0.017.
Values may be sent and summed in bfloat16 or wider, within the bound.
A program may use at most 64 MiB of HBM per device.

v0:
```python
import functools

import jax
import jax.numpy as jnp
from jax import lax
from jax.experimental import pallas as pl
from jax.experimental.pallas import tpu as pltpu
from jax.sharding import PartitionSpec as P

BLOCK = 128
CHUNK = 256
MESH = pl.DeviceIdType.MESH
F32 = jnp.float32
BF16 = jnp.bfloat16


def dot(a, b):
    return jnp.dot(a, b, preferred_element_type=F32)


def dot_rows(a, b):
    return lax.dot_general(a, b, (((1,), (1,)), ((), ())), preferred_element_type=F32)


def rounded(a, b):
    return dot(a.astype(BF16), b.astype(BF16))


def even_blocks(x, n):
    return jnp.concatenate([x[i:i + n] for i in range(0, x.shape[0], 2 * n)], axis=0)


def odd_blocks(x, n):
    return jnp.concatenate([x[i:i + n] for i in range(n, x.shape[0], 2 * n)], axis=0)


def interleave(even, odd, n):
    rows = []
    for i in range(0, even.shape[0], n):
        rows += [even[i:i + n], odd[i:i + n]]
    return jnp.concatenate(rows, axis=0)


def local_maps(
    base, lanes, blocks, dk, dv, reset_ref, k_ref, q_ref, v_ref, beta_ref,
    a_ref, d_ref, z_ref, send_ref,
):
    def columns(h, size):
        return pl.ds(pl.multiple_of((base + h) * size, size), size)

    row = lax.broadcasted_iota(jnp.int32, (BLOCK, BLOCK), 0)
    col = lax.broadcasted_iota(jnp.int32, (BLOCK, BLOCK), 1)
    diagonal = row == col
    eye = diagonal.astype(F32)
    items = [(h, b) for b in range(blocks) for h in range(lanes)]

    ks, qs, rks, rk_rows, rqs, betas, lows, scores = [], [], [], [], [], [], [], []
    for h, b in items:
        at = slice(b * BLOCK, (b + 1) * BLOCK)
        k = k_ref[at, columns(h, dk)]
        q = q_ref[at, columns(h, dk)]
        products = dot_rows(jnp.concatenate([k, q], axis=0), k)
        gram, cross = products[:BLOCK], products[BLOCK:]
        squares = jnp.where(diagonal, gram, 0.0)
        rk = lax.rsqrt(jnp.sum(squares, axis=1, keepdims=True) + 1e-6)
        rk_row = lax.rsqrt(jnp.sum(squares, axis=0, keepdims=True) + 1e-6)
        q32 = q.astype(F32)
        rq = lax.rsqrt(jnp.sum(q32 * q32, axis=1, keepdims=True) + 1e-6)
        every = beta_ref[:, at]
        wanted = lax.broadcasted_iota(jnp.int32, every.shape, 0) == base + h
        beta_row = jnp.sum(jnp.where(wanted, every, 0.0), axis=0, keepdims=True)
        beta = jnp.sum(jnp.where(diagonal, beta_row, 0.0), axis=1, keepdims=True)
        lows.append(jnp.where(row > col, gram * (beta * rk) * rk_row, 0.0))
        scores.append(jnp.where(row >= col, cross * rq, 0.0).astype(BF16))
        ks.append(k)
        qs.append(q)
        rks.append(rk)
        rk_rows.append(rk_row)
        rqs.append(rq)
        betas.append(beta_row)

    inv = []
    for low in lows:
        pairs = jnp.where((row // 2) == (col // 2), low, 0.0)
        cut = jnp.where(((row // 4) == (col // 4)) & ((row // 2) != (col // 2)), low, 0.0)
        inner = cut - pltpu.roll(cut, BLOCK - 1, 1) * jnp.sum(pairs, axis=0, keepdims=True)
        inner = inner - pltpu.roll(inner, 1, 0) * jnp.sum(pairs, axis=1, keepdims=True)
        inv.append(eye - pairs - inner)
    narrow = [x.astype(BF16) for x in inv]
    lows = [low.astype(BF16) for low in lows]
    n = 4
    while n < BLOCK:
        cut = ((row // (2 * n)) == (col // (2 * n))) & ((row // n) != (col // n))
        cut = jnp.where(cut, 1.0, 0.0).astype(BF16)
        if n < 16:
            inner = [dot(low * cut, x).astype(BF16) for low, x in zip(lows, narrow)]
            inv = [x - dot(y, z) for x, y, z in zip(inv, narrow, inner)]
            narrow = [x.astype(BF16) for x in inv]
        else:
            below = odd_blocks(cut, n)
            inner = [
                dot(odd_blocks(low, n) * below, x).astype(BF16) for low, x in zip(lows, narrow)
            ]
            inner = [interleave(jnp.zeros_like(x), x, n) for x in inner]
            changed = [
                odd_blocks(x, n) - dot(odd_blocks(y, n), z)
                for x, y, z in zip(inv, narrow, inner)
            ]
            inv = [interleave(even_blocks(x, n), y, n) for x, y in zip(inv, changed)]
            narrow = [
                interleave(even_blocks(x, n), y.astype(BF16), n) for x, y in zip(narrow, changed)
            ]
        n *= 2

    solved = []
    for (h, b), k, x, rk, rk_row, beta in zip(items, ks, inv, rks, rk_rows, betas):
        v = v_ref[b * BLOCK:(b + 1) * BLOCK, columns(h, dv)]
        scaled = x * beta
        solved.append(
            jnp.concatenate(
                [rk * rounded(scaled * rk_row, k), rk * rounded(scaled, v)], axis=1
            ).astype(BF16)
        )
    parts = [
        dot(jnp.concatenate([k.T, score], axis=0), wu)
        for k, score, wu in zip(ks, scores, solved)
    ]

    zs = [None] * lanes
    for (h, b), q, rq, part in zip(items, qs, rqs, parts):
        kept = jnp.float32(1.0)
        for slot in range(reset_ref.shape[1]):
            kept = jnp.where(reset_ref[0, slot] == b, 0.0, kept)
        take = part[:dk, :dk]
        read = rq * q.astype(F32) - part[dk:, :dk]
        if b == 0:
            linear = kept * (eye - take)
            constant = part[:dk, dk:]
            out_linear = kept * read
            out_constant = part[dk:, dk:]
        else:
            z = zs[h] * kept
            moved = rounded(jnp.concatenate([take, read], axis=0), z)
            linear = z[:, :dk] - moved[:dk, :dk]
            constant = z[:, dk:] - moved[:dk, dk:] + part[:dk, dk:]
            out_linear = moved[dk:, :dk]
            out_constant = moved[dk:, dk:] + part[dk:, dk:]
        zs[h] = jnp.concatenate([linear, constant], axis=1)
        a_ref[base + h, b * BLOCK:(b + 1) * BLOCK] = out_linear.astype(BF16)
        d_ref[base + h, b * BLOCK:(b + 1) * BLOCK] = out_constant.astype(BF16)
    for h in range(lanes):
        z_ref[base + h] = zs[h][:, dk:]
        send_ref[base + h] = zs[h].astype(BF16)


def layer_kernel(
    shards, groups, heads, dk, dv, chunks,
    reset_ref, k_ref, q_ref, v_ref, beta_ref, w_ref, out_ref,
    a_ref, d_ref, z_ref, zb_ref,
    w_vmem, before, joined, chain, came, goes, hands, normed, give1, take1, kept, give2, take2, own,
    w_sem, pair_send, pair_recv, chain_send, chain_recv, step_send, step_recv, send1, recv1, send2, recv2,
):
    tokens = k_ref.shape[0]
    rows = tokens // groups
    pairs = groups // 2
    half = pairs * rows
    s = lax.axis_index("seq")
    g = lax.axis_index("head")
    y, c = g // 2, g % 2
    mate = y * 2 + (1 - c)

    for j in range(chunks):
        pltpu.make_async_copy(
            w_ref.at[:, pl.ds(j * CHUNK, CHUNK)], w_vmem.at[j], w_sem.at[j]
        ).start()

    share = heads // 2
    parity = s % 2
    odd = parity == 1
    partner = s + 1 - 2 * parity

    def mine(i):
        return (1 - parity) * share + i

    def theirs(i):
        return parity * share + i

    barrier = pltpu.get_barrier_semaphore()

    def greet(**place):
        pl.semaphore_signal(barrier, inc=1, device_id=place, device_id_type=MESH)

    for gap in (1, 2):
        @pl.when(s >= gap)
        def _():
            greet(seq=s - gap)

        @pl.when(s < shards - gap)
        def _():
            greet(seq=s + gap)

    greet(head=mate)
    for step in range(1, pairs):
        greet(head=((y + step) % pairs) * 2 + c)
    def to_partner(i):
        return pltpu.make_async_remote_copy(
            src_ref=zb_ref.at[theirs(i)], dst_ref=before.at[i],
            send_sem=pair_send.at[i], recv_sem=pair_recv.at[i],
            device_id={"seq": partner}, device_id_type=MESH,
        )

    def to_chain(i):
        return pltpu.make_async_remote_copy(
            src_ref=goes.at[i], dst_ref=chain.at[i],
            send_sem=chain_send.at[i], recv_sem=chain_recv.at[i],
            device_id={"seq": jnp.minimum(s + 2, shards - 1)}, device_id_type=MESH,
        )

    def to_next(i):
        return pltpu.make_async_remote_copy(
            src_ref=hands.at[i], dst_ref=came.at[i],
            send_sem=step_send.at[i], recv_sem=step_recv.at[i],
            device_id={"seq": jnp.minimum(s + 1, shards - 1)}, device_id_type=MESH,
        )

    def maps(turn, carry):
        local_maps(
            jnp.where(turn == 0, theirs(0), mine(0)), share, tokens // BLOCK, dk, dv,
            reset_ref, k_ref, q_ref, v_ref, beta_ref, a_ref, d_ref, z_ref, zb_ref,
        )

        @pl.when(turn == 0)
        def _():
            pl.semaphore_wait(
                barrier,
                pairs
                + jnp.where(s >= 1, 1, 0) + jnp.where(s >= 2, 1, 0)
                + jnp.where(s < shards - 1, 1, 0) + jnp.where(s < shards - 2, 1, 0),
            )
            for i in range(share):
                to_partner(i).start()

        return carry

    lax.fori_loop(0, 2, maps, 0)

    def replay(h, memory):
        attended = dot(a_ref[h], memory) + d_ref[h].astype(F32)
        scale = lax.rsqrt(jnp.mean(attended * attended, axis=1, keepdims=True) + 1e-5)
        result = (attended * scale).astype(BF16)
        columns = pl.ds(pl.multiple_of(h * dv, dv), dv)
        for t in range(groups):
            place = jnp.where(c == t % 2, half, 0) + (t // 2) * rows
            normed[pl.ds(pl.multiple_of(place, rows), rows), columns] = result[
                t * rows:(t + 1) * rows
            ]

    for i in range(share):
        h = mine(i)
        to_partner(i).wait_recv()

        @pl.when(odd)
        def _():
            both = dot(zb_ref[h, :, :dk], before[i])
            joined[i, :, :dk] = both[:, :dk]
            joined[i, :, dk:] = both[:, dk:] + z_ref[h]

        @pl.when(jnp.logical_not(odd))
        def _():
            both = dot(before[i, :, :dk], zb_ref[h])
            joined[i, :, :dk] = both[:, :dk]
            joined[i, :, dk:] = both[:, dk:] + before[i, :, dk:].astype(F32)

        @pl.when(s < 2)
        def _():
            chain[i] = jnp.zeros((dk, dv), BF16)

        @pl.when(s >= 2)
        def _():
            to_chain(i).wait_recv()

        goes[i] = (
            dot(joined[i, :, :dk].astype(BF16), chain[i]) + joined[i, :, dk:]
        ).astype(BF16)

        @pl.when(s < shards - 2)
        def _():
            to_chain(i).start()

        @pl.when(odd)
        def _():
            hands[i] = goes[i]
            joined[i, :, dk:] = (
                dot(before[i, :, :dk], chain[i]) + before[i, :, dk:].astype(F32)
            )

        @pl.when(jnp.logical_not(odd))
        def _():
            hands[i] = (dot(zb_ref[h, :, :dk], chain[i]) + z_ref[h]).astype(BF16)
            joined[i, :, dk:] = chain[i].astype(F32)

        @pl.when(s < shards - 1)
        def _():
            to_next(i).start()

    for i in range(share):
        replay(mine(i), joined[i, :, dk:].astype(BF16))

    for i in range(share):
        @pl.when(s == 0)
        def _():
            came[i] = jnp.zeros((dk, dv), BF16)

        @pl.when(s > 0)
        def _():
            to_next(i).wait_recv()

        replay(theirs(i), came[i])

    def first(j):
        return pltpu.make_async_remote_copy(
            src_ref=give1.at[j], dst_ref=take1.at[j],
            send_sem=send1.at[j], recv_sem=recv1.at[j],
            device_id={"head": mate}, device_id_type=MESH,
        )

    def second(j, step):
        other = (y + step) % pairs
        return pltpu.make_async_remote_copy(
            src_ref=give2.at[j, step - 1], dst_ref=take2.at[j, step - 1],
            send_sem=send2.at[j, step - 1], recv_sem=recv2.at[j, step - 1],
            device_id={"head": other * 2 + c}, device_id_type=MESH,
        )

    def pass_on(j):
        first(j).wait_recv()
        for step in range(1, pairs):
            at = pl.ds(pl.multiple_of(((y + step) % pairs) * rows, rows), rows)
            give2[j, step - 1] = (kept[j, at] + take1[j, at].astype(F32)).astype(BF16)
            second(j, step).start()
        at = pl.ds(pl.multiple_of(y * rows, rows), rows)
        own[j] = kept[j, at] + take1[j, at].astype(F32)

    def project(j, carry):
        pltpu.make_async_copy(
            w_ref.at[:, pl.ds(j * CHUNK, CHUNK)], w_vmem.at[j], w_sem.at[j]
        ).wait()
        part = dot(normed[...], w_vmem[j])
        give1[j] = part[:half].astype(BF16)
        first(j).start()
        kept[j] = part[half:]

        @pl.when(j > 0)
        def _():
            pass_on(j - 1)

        return carry

    lax.fori_loop(0, chunks, project, 0)
    pass_on(chunks - 1)

    for j in range(chunks):
        total = own[j]
        for step in range(1, pairs):
            second(j, step).wait_recv()
            total = total + take2[j, step - 1].astype(F32)
        out_ref[:, j * CHUNK:(j + 1) * CHUNK] = total.astype(BF16)

    for j in range(chunks):
        first(j).wait_send()
        for step in range(1, pairs):
            second(j, step).wait_send()

    for i in range(share):
        to_partner(i).wait_send()

    @pl.when(s < shards - 2)
    def _():
        for i in range(share):
            to_chain(i).wait_send()

    @pl.when(s < shards - 1)
    def _():
        for i in range(share):
            to_next(i).wait_send()


def layer(resets, k, q, v, beta, w, shards, groups, heads, dk, dv):
    tokens = k.shape[0]
    width = w.shape[1]
    chunks = width // CHUNK
    rows = tokens // groups
    pairs = groups // 2
    half = pairs * rows
    far = max(pairs - 1, 1)
    share = heads // 2
    vmem = pl.BlockSpec(memory_space=pltpu.VMEM)
    dma = pltpu.SemaphoreType.DMA
    return pl.pallas_call(
        functools.partial(layer_kernel, shards, groups, heads, dk, dv, chunks),
        in_specs=[
            pl.BlockSpec(memory_space=pltpu.SMEM), vmem, vmem, vmem, vmem,
            pl.BlockSpec(memory_space=pl.ANY),
        ],
        out_specs=vmem,
        out_shape=jax.ShapeDtypeStruct((rows, width), BF16),
        scratch_shapes=[
            pltpu.VMEM((heads, tokens, dk), BF16),
            pltpu.VMEM((heads, tokens, dv), BF16),
            pltpu.VMEM((heads, dk, dv), F32),
            pltpu.VMEM((heads, dk, dk + dv), BF16),
            pltpu.VMEM((chunks, w.shape[0], CHUNK), BF16),
            pltpu.VMEM((share, dk, dk + dv), BF16),
            pltpu.VMEM((share, dk, dk + dv), F32),
            pltpu.VMEM((share, dk, dv), BF16),
            pltpu.VMEM((share, dk, dv), BF16),
            pltpu.VMEM((share, dk, dv), BF16),
            pltpu.VMEM((share, dk, dv), BF16),
            pltpu.VMEM((tokens, heads * dv), BF16),
            pltpu.VMEM((chunks, half, CHUNK), BF16),
            pltpu.VMEM((chunks, half, CHUNK), BF16),
            pltpu.VMEM((chunks, half, CHUNK), F32),
            pltpu.VMEM((chunks, far, rows, CHUNK), BF16),
            pltpu.VMEM((chunks, far, rows, CHUNK), BF16),
            pltpu.VMEM((chunks, rows, CHUNK), F32),
            dma((chunks,)),
            dma((share,)),
            dma((share,)),
            dma((share,)),
            dma((share,)),
            dma((share,)),
            dma((share,)),
            dma((chunks,)),
            dma((chunks,)),
            dma((chunks, far)),
            dma((chunks, far)),
        ],
        compiler_params=pltpu.CompilerParams(
            collective_id=0, has_side_effects=True, vmem_limit_bytes=36 * 1024 * 1024
        ),
        name="layer",
    )(resets, k, q, v, beta, w)


def body(shards, groups, queries, keys, values, beta, reset_blocks, out_weight):
    tokens, heads, dk = queries.shape
    dv = values.shape[2]
    return layer(
        reset_blocks,
        keys.reshape(tokens, heads * dk),
        queries.reshape(tokens, heads * dk),
        values.reshape(tokens, heads * dv),
        beta,
        out_weight,
        shards, groups, heads, dk, dv,
    )


def solution(mesh):
    return jax.shard_map(
        functools.partial(body, mesh.shape["seq"], mesh.shape["head"]),
        mesh=mesh,
        in_specs=(
            P("seq", "head", None),
            P("seq", "head", None),
            P("seq", "head", None),
            P("head", "seq"),
            P("seq", None),
            P("head", None),
        ),
        out_specs=P(("seq", "head"), None),
        check_vma=False,
    )
```

profile of v0, /device:TPU:27, one launch (start us, length us, event | category | flops | bytes accessed | tf_op | source)
XLA Modules:
  0.0 60.8 jit_solution(13348537008318308018)
XLA Ops:
  0.0 1.4 %copy.9 = bf16[64,8,4,256]{3,1,2,0:T(8,128)(2,1)S(1)} copy(bf16[64,8,4,256]{3,2,1,0:T(4,128)(2,1)} %bitcast.9) | data formatting | bytes 2097152
  1.4 1.4 %copy_bitcast_fusion = (bf16[512,512]{1,0:T(8,128)(2,1)S(1)}, bf16[512,512]{1,0:T(8,128)(2,1)S(1)}) fusion(bf16[64,8,4,128]{3,2,1,0:T(4,128)(2,1)} %bitcast.10, bf16[64,8,4,128]{3,2,1,0:T(4,128)(2,1)} %bitcast.11), kind=kLoop, calls=%fused_computation | loop fusion | bytes 2097152 | tf_op jit(solution)/shard_map/reshape | solution.py:451
  2.8 0.0 copy-start
  2.8 3.4 %copy-done = bf16[1024,4096]{1,0:T(8,128)(2,1)S(1)} copy-done((bf16[1024,4096]{1,0:T(8,128)(2,1)S(1)}, bf16[1024,4096]{1,0:T(8,128)(2,1)}, u32[]{:S(2)}) %copy-start) | copy-done | bytes 8388632
  6.2 0.0 copy-start.1
  6.2 0.7 %copy-done.1 = f32[4,512]{1,0:T(4,128)S(1)} copy-done((f32[4,512]{1,0:T(4,128)S(1)}, f32[4,512]{1,0:T(4,128)}, u32[]{:S(2)}) %copy-start.1) | copy-done | bytes 8216
  6.9 0.0 copy-start.2
  6.9 0.7 %copy-done.2 = s32[1,2]{1,0:T(1,128)S(1)} copy-done((s32[1,2]{1,0:T(1,128)S(1)}, s32[1,2]{1,0:T(1,128)}, u32[]{:S(2)}) %copy-start.2) | copy-done | bytes 32
  7.5 52.3 %layer.1 = bf16[128,4096]{1,0:T(8,128)(2,1)S(1)} custom-call(s32[1,2]{1,0:T(1,128)S(1)} %copy-done.2, bf16[512,512]{1,0:T(8,128)(2,1)S(1)} %get-tuple-element.6.k_ref, bf16[512,512]{1,0:T(8,128)(2,1)S(1)} %get-tuple-element.5.q_ref, bf16[512,1024]{1,0:T(8,128)(2,1)S(1)} %bitcast.8, f32[4,512]{1,0:T(4,128)S(1)} %copy-done.1, bf16[1024,4096]{1,0:T(8,128)(2,1)S(1)} %copy-done), custom_call_target="tpu_custom_call" | custom-call | tf_op jit(solution)/shard_map/layer/pallas_call | solution.py:399
  59.8 1.0 %copy.13 = bf16[128,4096]{1,0:T(8,128)(2,1)} copy(bf16[128,4096]{1,0:T(8,128)(2,1)S(1)} %layer.1) | data formatting | bytes 2097152
Async XLA Ops:
  2.8 3.4 %copy-start = (bf16[1024,4096]{1,0:T(8,128)(2,1)S(1)}, bf16[1024,4096]{1,0:T(8,128)(2,1)}, u32[]{:S(2)}) copy-start(bf16[1024,4096]{1,0:T(8,128)(2,1)} %w_ref.1) | copy-start | bytes 25165828
  6.2 0.7 %copy-start.1 = (f32[4,512]{1,0:T(4,128)S(1)}, f32[4,512]{1,0:T(4,128)}, u32[]{:S(2)}) copy-start(f32[4,512]{1,0:T(4,128)} %beta_ref.1) | copy-start | bytes 24580
  6.9 0.7 %copy-start.2 = (s32[1,2]{1,0:T(1,128)S(1)}, s32[1,2]{1,0:T(1,128)}, u32[]{:S(2)}) copy-start(s32[1,2]{1,0:T(1,128)} %reset_ref.1) | copy-start | bytes 28
where the time goes:
time: 61.3 us; the launch traced here: 60.8 us
  Pallas kernels  52.3 us (85%)
  local copies, waits for them, and re-layouts  8.49 us (14%)
    pallas_call x1, Pallas kernels, layer(): pl.pallas_call(functools.partial(layer_kernel, shards, groups, heads, dk,...  52.3 us
    unnamed x8, local copies, waits for them, and re-layouts  7.14 us
    reshape x1, local copies, waits for them, and re-layouts, body(): queries.reshape(tokens, heads * dk)  1.35 us

commit v1 on v0

--- a/solution.py
+++ b/solution.py
@@ -9,6 +9,7 @@
 
 BLOCK = 128
 CHUNK = 256
+LANES = 128
 MESH = pl.DeviceIdType.MESH
 F32 = jnp.float32
 BF16 = jnp.bfloat16
@@ -45,9 +46,10 @@
     base, lanes, blocks, dk, dv, reset_ref, k_ref, q_ref, v_ref, beta_ref,
     a_ref, d_ref, z_ref, send_ref,
 ):
-    def columns(h, size):
-        return pl.ds(pl.multiple_of((base + h) * size, size), size)
-
+    def take(ref, b, h, every):
+        return ref[pl.ds(b * BLOCK * every + h, BLOCK, stride=every), :]
+
+    heads = beta_ref.shape[0]
     row = lax.broadcasted_iota(jnp.int32, (BLOCK, BLOCK), 0)
     col = lax.broadcasted_iota(jnp.int32, (BLOCK, BLOCK), 1)
     diagonal = row == col
@@ -57,14 +59,14 @@
     ks, qs, rks, rk_rows, rqs, betas, lows, scores = [], [], [], [], [], [], [], []
     for h, b in items:
         at = slice(b * BLOCK, (b + 1) * BLOCK)
-        k = k_ref[at, columns(h, dk)]
-        q = q_ref[at, columns(h, dk)]
+        k = take(k_ref, b, base + h, heads).astype(BF16)
+        q32 = take(q_ref, b, base + h, heads)
+        q = q32.astype(BF16)
         products = dot_rows(jnp.concatenate([k, q], axis=0), k)
         gram, cross = products[:BLOCK], products[BLOCK:]
         squares = jnp.where(diagonal, gram, 0.0)
         rk = lax.rsqrt(jnp.sum(squares, axis=1, keepdims=True) + 1e-6)
         rk_row = lax.rsqrt(jnp.sum(squares, axis=0, keepdims=True) + 1e-6)
-        q32 = q.astype(F32)
         rq = lax.rsqrt(jnp.sum(q32 * q32, axis=1, keepdims=True) + 1e-6)
         every = beta_ref[:, at]
         wanted = lax.broadcasted_iota(jnp.int32, every.shape, 0) == base + h
@@ -114,7 +116,10 @@
 
     solved = []
     for (h, b), k, x, rk, rk_row, beta in zip(items, ks, inv, rks, rk_rows, betas):
-        v = v_ref[b * BLOCK:(b + 1) * BLOCK, columns(h, dv)]
+        pieces = dv // LANES
+        v = jnp.concatenate(
+            [take(v_ref, b, base + h + heads * i, heads * pieces) for i in range(pieces)], axis=1
+        )
         scaled = x * beta
         solved.append(
             jnp.concatenate(
@@ -131,16 +136,16 @@
         kept = jnp.float32(1.0)
         for slot in range(reset_ref.shape[1]):
             kept = jnp.where(reset_ref[0, slot] == b, 0.0, kept)
-        take = part[:dk, :dk]
+        pull = part[:dk, :dk]
         read = rq * q.astype(F32) - part[dk:, :dk]
         if b == 0:
-            linear = kept * (eye - take)
+            linear = kept * (eye - pull)
             constant = part[:dk, dk:]
             out_linear = kept * read
             out_constant = part[dk:, dk:]
         else:
             z = zs[h] * kept
-            moved = rounded(jnp.concatenate([take, read], axis=0), z)
+            moved = rounded(jnp.concatenate([pull, read], axis=0), z)
             linear = z[:, :dk] - moved[:dk, :dk]
             constant = z[:, dk:] - moved[:dk, dk:] + part[:dk, dk:]
             out_linear = moved[dk:, :dk]
@@ -155,12 +160,12 @@
 
 def layer_kernel(
     shards, groups, heads, dk, dv, chunks,
-    reset_ref, k_ref, q_ref, v_ref, beta_ref, w_ref, out_ref,
-    a_ref, d_ref, z_ref, zb_ref,
+    reset_hbm, k_rows, q_rows, v_rows, beta_hbm, w_ref, out_ref,
+    k_ref, q_ref, v_ref, reset_ref, beta_ref, a_ref, d_ref, z_ref, zb_ref,
     w_vmem, before, joined, chain, came, goes, hands, normed, give1, take1, kept, give2, take2, own,
-    w_sem, pair_send, pair_recv, chain_send, chain_recv, step_send, step_recv, send1, recv1, send2, recv2,
+    small_sem, w_sem, pair_send, pair_recv, chain_send, chain_recv, step_send, step_recv, send1, recv1, send2, recv2,
 ):
-    tokens = k_ref.shape[0]
+    tokens = beta_hbm.shape[1]
     rows = tokens // groups
     pairs = groups // 2
     half = pairs * rows
@@ -169,6 +174,12 @@
     y, c = g // 2, g % 2
     mate = y * 2 + (1 - c)
 
+    small = [
+        pltpu.make_async_copy(beta_hbm, beta_ref, small_sem.at[0]),
+        pltpu.make_async_copy(reset_hbm, reset_ref, small_sem.at[1]),
+    ]
+    for copy in small:
+        copy.start()
     for j in range(chunks):
         pltpu.make_async_copy(
             w_ref.at[:, pl.ds(j * CHUNK, CHUNK)], w_vmem.at[j], w_sem.at[j]
@@ -242,6 +253,10 @@
 
         return carry
 
+    for wide, packed in ((k_ref, k_rows), (q_ref, q_rows), (v_ref, v_rows)):
+        wide[...] = packed[...].astype(F32)
+    for copy in small:
+        copy.wait()
     lax.fori_loop(0, 2, maps, 0)
 
     def replay(h, memory):
@@ -386,7 +401,7 @@
 
 
 def layer(resets, k, q, v, beta, w, shards, groups, heads, dk, dv):
-    tokens = k.shape[0]
+    tokens = beta.shape[1]
     width = w.shape[1]
     chunks = width // CHUNK
     rows = tokens // groups
@@ -395,16 +410,19 @@
     far = max(pairs - 1, 1)
     share = heads // 2
     vmem = pl.BlockSpec(memory_space=pltpu.VMEM)
+    hbm = pl.BlockSpec(memory_space=pltpu.HBM)
     dma = pltpu.SemaphoreType.DMA
     return pl.pallas_call(
         functools.partial(layer_kernel, shards, groups, heads, dk, dv, chunks),
-        in_specs=[
-            pl.BlockSpec(memory_space=pltpu.SMEM), vmem, vmem, vmem, vmem,
-            pl.BlockSpec(memory_space=pl.ANY),
-        ],
+        in_specs=[hbm, vmem, vmem, vmem, hbm, hbm],
         out_specs=vmem,
         out_shape=jax.ShapeDtypeStruct((rows, width), BF16),
         scratch_shapes=[
+            pltpu.VMEM(k.shape, F32),
+            pltpu.VMEM(q.shape, F32),
+            pltpu.VMEM(v.shape, F32),
+            pltpu.SMEM(resets.shape, resets.dtype),
+            pltpu.VMEM(beta.shape, beta.dtype),
             pltpu.VMEM((heads, tokens, dk), BF16),
             pltpu.VMEM((heads, tokens, dv), BF16),
             pltpu.VMEM((heads, dk, dv), F32),
@@ -423,6 +441,7 @@
             pltpu.VMEM((chunks, far, rows, CHUNK), BF16),
             pltpu.VMEM((chunks, far, rows, CHUNK), BF16),
             pltpu.VMEM((chunks, rows, CHUNK), F32),
+            dma((2,)),
             dma((chunks,)),
             dma((share,)),
             dma((share,)),
@@ -436,7 +455,7 @@
             dma((chunks, far)),
         ],
         compiler_params=pltpu.CompilerParams(
-            collective_id=0, has_side_effects=True, vmem_limit_bytes=36 * 1024 * 1024
+            collective_id=0, has_side_effects=True, vmem_limit_bytes=56 * 1024 * 1024
         ),
         name="layer",
     )(resets, k, q, v, beta, w)
@@ -447,9 +466,11 @@
     dv = values.shape[2]
     return layer(
         reset_blocks,
-        keys.reshape(tokens, heads * dk),
-        queries.reshape(tokens, heads * dk),
-        values.reshape(tokens, heads * dv),
+        keys.reshape(tokens * heads, dk),
+        queries.reshape(tokens * heads, dk),
+        values.reshape(tokens, heads, dv // LANES, LANES)
+        .transpose(0, 2, 1, 3)
+        .reshape(tokens * (dv // LANES) * heads, LANES),
         beta,
         out_weight,
         shards, groups, heads, dk, dv,

time: 61.3 us -> 58.9 us (0.961)
  local copies, waits for them, and re-layouts: 8.49 us -> 2.29 us
  Pallas kernels: 52.3 us -> 56.1 us
    unnamed x8 -> x1, local copies, waits for them, and re-layouts: 7.14 us -> 2.29 us
    pallas_call x1, Pallas kernels: 52.3 us -> 56.1 us  [layer(): pl.pallas_call(functools.partial(layer_kernel, shards, groups, heads, dk,...]
    reshape x1 -> x0, local copies, waits for them, and re-layouts: 1.35 us -> none  [body(): queries.reshape(tokens, heads * dk)]
where the time goes in v1:
time: 58.9 us; the launch traced here: 58.4 us
  Pallas kernels  56.1 us (95%)
  local copies, waits for them, and re-layouts  2.29 us (4%)
    pallas_call x1, Pallas kernels, layer(): pl.pallas_call(functools.partial(layer_kernel, shards, groups, heads, dk,...  56.1 us
    unnamed x1, local copies, waits for them, and re-layouts  2.29 us

profile of v1, /device:TPU:27, one launch (start us, length us, event | category | flops | bytes accessed | tf_op | source)
XLA Modules:
  0.0 58.4 jit_solution(12520681836799442710)
XLA Ops:
  0.0 56.1 %layer.1 = bf16[128,4096]{1,0:T(8,128)(2,1)} custom-call(s32[1,2]{1,0:T(1,128)} %reset_hbm.1, bf16[2048,128]{1,0:T(8,128)(2,1)} %bitcast.8, bf16[2048,128]{1,0:T(8,128)(2,1)} %bitcast.9, bf16[4096,128]{1,0:T(8,128)(2,1)} %bitcast.7, f32[4,512]{1,0:T(4,128)} %beta_hbm.1, bf16[1024,4096]{1,0:T(8,128)(2,1)} %w_ref.1), custom_call_target="tpu_custom_call" | custom-call | tf_op jit(solution)/shard_map/layer/pallas_call | solution.py:415
  56.1 2.3 %copy.9 = bf16[128,4096]{1,0:T(8,128)(2,1)} copy(bf16[128,4096]{1,0:T(8,128)(2,1)} %layer.1) | data formatting | bytes 2097152

commit v2 on v1

--- a/solution.py
+++ b/solution.py
@@ -302,6 +302,9 @@
         def _():
             to_chain(i).start()
 
+    for i in range(share):
+        h = mine(i)
+
         @pl.when(odd)
         def _():
             hands[i] = goes[i]
@@ -360,10 +363,9 @@
         pltpu.make_async_copy(
             w_ref.at[:, pl.ds(j * CHUNK, CHUNK)], w_vmem.at[j], w_sem.at[j]
         ).wait()
-        part = dot(normed[...], w_vmem[j])
-        give1[j] = part[:half].astype(BF16)
+        give1[j] = dot(normed[:half], w_vmem[j]).astype(BF16)
         first(j).start()
-        kept[j] = part[half:]
+        kept[j] = dot(normed[half:], w_vmem[j])
 
         @pl.when(j > 0)
         def _():

time: 58.9 us -> 59.3 us (level)
  no operation moved by 1% of the time
where the time goes in v2:
time: 59.3 us; the launch traced here: 58.9 us
  Pallas kernels  56.6 us (95%)
  local copies, waits for them, and re-layouts  2.29 us (4%)
    pallas_call x1, Pallas kernels, layer(): pl.pallas_call(functools.partial(layer_kernel, shards, groups, heads, dk,...  56.6 us
    unnamed x1, local copies, waits for them, and re-layouts  2.29 us

profile of v2, /device:TPU:27, one launch (start us, length us, event | category | flops | bytes accessed | tf_op | source)
XLA Modules:
  0.0 58.9 jit_solution(13651828999456660765)
XLA Ops:
  0.0 56.6 %layer.1 = bf16[128,4096]{1,0:T(8,128)(2,1)} custom-call(s32[1,2]{1,0:T(1,128)} %reset_hbm.1, bf16[2048,128]{1,0:T(8,128)(2,1)} %bitcast.8, bf16[2048,128]{1,0:T(8,128)(2,1)} %bitcast.9, bf16[4096,128]{1,0:T(8,128)(2,1)} %bitcast.7, f32[4,512]{1,0:T(4,128)} %beta_hbm.1, bf16[1024,4096]{1,0:T(8,128)(2,1)} %w_ref.1), custom_call_target="tpu_custom_call" | custom-call | tf_op jit(solution)/shard_map/layer/pallas_call | solution.py:417
  56.6 2.3 %copy.9 = bf16[128,4096]{1,0:T(8,128)(2,1)} copy(bf16[128,4096]{1,0:T(8,128)(2,1)} %layer.1) | data formatting | bytes 2097152
